TPU v7x, 512 devices: a whole 4x8x8 slice. The times are simulated.
512 devices in a mesh: clip: 64 (over z_hi, y, x), space: 8 (over z_lo, core).
Axes of the slice: x: 4, y: 8, z: 8 (z_hi: 2, z_lo: 4; z = z_hi * 4 + z_lo), core: 2. Of those that a mesh axis runs over, the one named last changes fastest.
Arguments:
- latent: bfloat16 [512, 256, 640], P('clip', 'space'), may hold values from -6 to 6
- spatial_qkv: bfloat16 [640, 960], replicated, may hold values from -2.1875 to 2.1875
- spatial_out: bfloat16 [320, 640], replicated, may hold values from -0.3125 to 0.3125
- temporal_qkv: bfloat16 [640, 960], replicated, may hold values from -2.1875 to 2.1875
- temporal_out: bfloat16 [320, 640], replicated, may hold values from -0.3125 to 0.3125
Outputs:
- latent_out: bfloat16 [512, 256, 640], P('clip', 'space')
All inputs are finite; a program needn't handle non-finite values.
Results may differ from a plain program's by a relative error of at most 0.012.
Values may be sent and summed in bfloat16 or wider, within the bound.
A program may use at most 128 MiB of HBM per device.

v0:
```python
import jax
import jax.numpy as jnp
from jax import lax
from jax.sharding import PartitionSpec as P

HEADS = 5
CTX = 2


def padded(cells, sides, width):
    for axis, dim in sides:
        count = lax.axis_size(axis)
        ends = count - 1
        head = lax.slice_in_dim(cells, 0, width, axis=dim)
        tail = lax.slice_in_dim(cells, cells.shape[dim] - width, cells.shape[dim], axis=dim)
        cells = jnp.concatenate(
            [
                lax.ppermute(tail, axis, [(i, (i + 1) % count) for i in range(ends)]),
                cells,
                lax.ppermute(head, axis, [((i + 1) % count, i) for i in range(ends)]),
            ],
            axis=dim,
        )
    return cells


def normalize(values):
    widened = values.astype(jnp.float32)
    center = widened - jnp.mean(widened, axis=-1, keepdims=True)
    spread = jnp.mean(center * center, axis=-1, keepdims=True)
    return (center * lax.rsqrt(spread + 1e-05)).astype(jnp.bfloat16)


def project(values, weight):
    flat_rows = values.reshape(-1, values.shape[-1])
    output = jnp.dot(flat_rows, weight, preferred_element_type=jnp.float32)
    return output.reshape(values.shape[:-1] + (weight.shape[1],))


def attend_space(queries, key_value):
    frame_count, row_count, inner_width = queries.shape
    key_count = key_value.shape[1]
    head_dim = inner_width // HEADS
    query_heads = queries.reshape(frame_count, row_count, HEADS, head_dim)
    key_heads = key_value[..., :inner_width].reshape(frame_count, key_count, HEADS, head_dim)
    value_heads = key_value[..., inner_width:].reshape(frame_count, key_count, HEADS, head_dim)
    scores = jnp.einsum(
        "fqhd,fkhd->fhqk", query_heads, key_heads, preferred_element_type=jnp.float32
    ) * head_dim ** (-0.5)
    weights = jax.nn.softmax(scores, axis=-1).astype(jnp.bfloat16)
    mixed = jnp.einsum("fhqk,fkhd->fqhd", weights, value_heads, preferred_element_type=jnp.float32)
    return mixed.astype(jnp.bfloat16).reshape(frame_count, row_count, inner_width)


def attend_time(queries, key_value, allowed):
    frame_count, row_count, inner_width = queries.shape
    key_count = key_value.shape[0]
    head_dim = inner_width // HEADS
    query_heads = queries.reshape(frame_count, row_count, HEADS, head_dim)
    key_heads = key_value[..., :inner_width].reshape(key_count, row_count, HEADS, head_dim)
    value_heads = key_value[..., inner_width:].reshape(key_count, row_count, HEADS, head_dim)
    scores = jnp.einsum(
        "fphd,kphd->phfk", query_heads, key_heads, preferred_element_type=jnp.float32
    ) * head_dim ** (-0.5)
    scores = jnp.where(allowed, scores, -1e30)
    weights = jax.nn.softmax(scores, axis=-1).astype(jnp.bfloat16)
    mixed = jnp.einsum("phfk,kphd->fphd", weights, value_heads, preferred_element_type=jnp.float32)
    return mixed.astype(jnp.bfloat16).reshape(frame_count, row_count, inner_width)


def body(latent, spatial_qkv, spatial_out, temporal_qkv, temporal_out):
    inner_width = spatial_out.shape[0]
    frame_count, row_count, channels = latent.shape
    packed = project(normalize(latent), spatial_qkv).astype(jnp.bfloat16)
    gathered = lax.all_gather(packed[..., inner_width:], "space", axis=1, tiled=True)
    mixed = attend_space(packed[..., :inner_width], gathered)
    spatial = (latent.astype(jnp.float32) + project(mixed, spatial_out)).astype(jnp.bfloat16)
    packed_time = project(normalize(spatial), temporal_qkv).astype(jnp.bfloat16)
    key_value = packed_time[..., inner_width:]
    context = padded(key_value, (("clip", 0),), CTX)
    anchors = lax.all_gather(key_value[0:1], "clip", axis=0, tiled=True)
    keys_all = jnp.concatenate([context, anchors], axis=0)
    clip_index = lax.axis_index("clip")
    final_clip = lax.axis_size("clip") - 1
    key_slots = jnp.arange(keys_all.shape[0], dtype=jnp.int32)
    allowed = ((key_slots >= CTX) | (clip_index > 0)) & (
        (key_slots < frame_count + CTX)
        | (key_slots >= frame_count + 2 * CTX)
        | (clip_index < final_clip)
    )
    mixed_time = attend_time(packed_time[..., :inner_width], keys_all, allowed)
    return (spatial.astype(jnp.float32) + project(mixed_time, temporal_out)).astype(jnp.bfloat16)


def solution(mesh):
    in_specs = (P("clip", "space", None), P(), P(), P(), P())
    out_specs = P("clip", "space", None)
    return jax.shard_map(body, mesh=mesh, in_specs=in_specs, out_specs=out_specs, check_vma=False)
```

profile of v0, /device:TPU:1, one launch (start us, length us, event | category | flops | bytes accessed | tf_op | source)
XLA Modules:
  0.0 254.1 jit_solution(15934328115324520423)
XLA Ops:
  6.5 0.0 copy-start
  6.5 0.0 all-gather.3.cloned.1.call-start
  6.5 1.2 convert_reduce_fusion
  7.7 1.2 fusion.16
  9.0 0.0 copy-done
  9.0 1.6 convolution_convert_fusion.1
  10.6 0.9 slice.47
  11.5 0.0 all-gather.3.cloned.1.call-update
  11.5 0.0 all-gather.5.cloned.1.call-start
  11.6 0.2 reshape.61
  11.8 47.6 %all-gather.3.cloned.1.call-done = bf16[8,256,640]{2,1,0:T(8,128)(2,1)} async-done(((bf16[8,32,640]{2,1,0:T(8,128)(2,1)}), bf16[8,256,640]{2,1,0:T(8,128)(2,1)}) %all-gather.3.cloned.1.call-update) | async-done | bytes 2621456 | tf_op jit(solution)/shard_map/all_gather | solution.py:75
  59.4 3.9 %fusion.30 = (bf16[8,256,320]{2,1,0:T(8,128)(2,1)}, bf16[8,256,320]{2,1,0:T(8,128)(2,1)S(1)}) fusion(bf16[8,256,640]{2,1,0:T(8,128)(2,1)} %all-gather.3.cloned.1.call-done), kind=kLoop, calls=%fused_computation.49 | loop fusion | bytes 5242880 | tf_op jit(solution)/shard_map/slice | solution.py:45
  63.3 2.5 %copy.21 = bf16[8,256,320]{1,2,0:T(8,128)(2,1)} copy(bf16[8,256,320]{2,1,0:T(8,128)(2,1)} %get-tuple-element.7) | data formatting | bytes 2621440 | tf_op jit(solution)/shard_map/slice | solution.py:45
  65.8 1.6 convolution_multiply_fusion
  67.4 0.0 copy-start.1
  67.4 1.1 copy-done.1
  68.5 0.4 fusion.32
  68.9 1.6 copy.20
  70.5 4.4 %fusion.13 = bf16[8,32,5,64]{3,1,2,0:T(8,128)(2,1)S(1)} fusion(bf16[8,256,5,64]{1,3,2,0:T(8,128)(2,1)} %bitcast.35, f32[8,5,32]{2,1,0:T(8,128)S(1)} %fusion.32, f32[8,5,32,256]{3,2,1,0:T(8,128)} %copy-done.1), kind=kOutput, calls=%fused_computation.23 | convolution fusion | flops 43009536 | bytes 2790400 | tf_op jit(solution)/shard_map/fhqk,fkhd->fqhd/dot_general | solution.py:51
  74.9 0.0 copy-start.2
  75.0 0.0 copy-start.4
  75.0 0.2 copy.23
  75.2 0.3 dot_general.31
  75.5 0.5 copy-done.2
  75.9 0.1 copy-done.4
  76.1 0.0 copy-start.3
  76.1 0.4 fusion.33
  76.5 0.2 multiply_reduce_fusion
  76.7 0.6 copy-done.3
  77.3 0.6 convolution_convert_fusion
  78.0 0.7 slice.54
  78.7 0.0 all-gather.5.cloned.1.call-update
  78.7 0.1 fusion.31
  78.8 3.7 %collective-permute-start = (bf16[2,32,640]{2,1,0:T(8,128)(2,1)S(1)}, bf16[2,32,640]{2,1,0:T(8,128)(2,1)}, u32[]{:S(2)}, u32[]{:S(2)}) collective-permute-start(bf16[2,32,640]{2,1,0:T(8,128)(2,1)S(1)} %get-tuple-element.9), channel_id=1, source_target_pairs={{0,8},{8,16},{16,24},{24,32},{32,40},{40,48},{48,56},{56,64},{64,7... | collective-permute-start | bytes 245768 | tf_op jit(solution)/shard_map/ppermute | solution.py:18
  82.6 1.5 collective-permute-start.1
  84.1 0.2 slice.52
  84.2 3.5 %copy.25 = bf16[8,32,640]{0,2,1:T(8,128)(2,1)} copy(bf16[8,32,640]{2,1,0:T(8,128)(2,1)S(1)} %slice.52) | data formatting | bytes 655360 | tf_op jit(solution)/shard_map/slice | solution.py:79
  87.7 0.2 reshape.64
  88.0 0.0 collective-permute-done
  88.0 4.6 %copy.24 = bf16[2,32,640]{0,2,1:T(8,128)(2,1)} copy(bf16[2,32,640]{2,1,0:T(8,128)(2,1)} %collective-permute-done) | data formatting | bytes 163840 | tf_op jit(solution)/shard_map/ppermute | solution.py:18
  92.6 0.0 collective-permute-done.1
  92.6 3.6 %copy.26 = bf16[2,32,640]{0,2,1:T(8,128)(2,1)} copy(bf16[2,32,640]{2,1,0:T(8,128)(2,1)S(1)} %collective-permute-done.1) | data formatting | bytes 163840 | tf_op jit(solution)/shard_map/ppermute | solution.py:20
  96.2 124.5 %all-gather.5.cloned.1.call-done = bf16[64,32,640]{2,1,0:T(8,128)(2,1)} async-done(((bf16[1,32,640]{2,1,0:T(8,128)(2,1)}), bf16[64,32,640]{2,1,0:T(8,128)(2,1)}) %all-gather.5.cloned.1.call-update) | async-done | bytes 2621456 | tf_op jit(solution)/shard_map/all_gather | solution.py:81
  220.7 6.7 %copy.27 = bf16[64,32,640]{0,2,1:T(8,128)(2,1)} copy(bf16[64,32,640]{2,1,0:T(8,128)(2,1)} %all-gather.5.cloned.1.call-done) | data formatting | bytes 5242880 | tf_op jit(solution)/shard_map/all_gather | solution.py:81
  227.4 10.6 %pad_maximum_fusion = bf16[76,32,640]{0,2,1:T(8,128)(2,1)S(1)} fusion(bf16[64,32,640]{0,2,1:T(8,128)(2,1)} %copy.27, bf16[2,32,640]{0,2,1:T(8,128)(2,1)} %copy.26, bf16[8,32,640]{0,2,1:T(8,128)(2,1)} %copy.25, bf16[2,32,640]{0,2,1:T(8,128)(2,1)} %copy.24), kind=kLoop, calls=%fused_computation.2 | loop fusion | flops 12451840 | bytes 6225920 | tf_op jit(solution)/shard_map/concatenate | solution.py:82
  238.0 1.9 fusion.29
  239.9 0.8 fusion.6
  240.7 0.4 fusion.34
  241.2 4.0 %fusion.12 = bf16[8,32,5,64]{3,0,2,1:T(8,128)(2,1)S(1)} fusion(bf16[76,32,5,64]{0,3,2,1:T(8,128)(2,1)} %bitcast.34, f32[32,5,8]{2,1,0:T(8,128)S(1)} %fusion.34, f32[32,5,8,76]{3,2,1,0:T(8,128)S(1)} %fusion.6), kind=kOutput, calls=%fused_computation.22 | convolution fusion | flops 12826955 | bytes 2114560 | tf_op jit(solution)/shard_map/phfk,kphd->fphd/dot_general | solution.py:67
  245.2 0.0 copy-start.5
  245.2 0.1 copy.29
  245.3 0.3 dot_general.36
  245.6 0.6 copy-done.5
  246.2 1.1 fusion.10
  (7 shorter events, 0.1 us)
Async XLA Ops:
  6.5 2.4 copy-start
  6.5 52.8 %all-gather.3.cloned.1.call-start = ((), (), s32[]{:S(2)}) async-start(), calls=%async_computation | async-start | bytes 2949120 | tf_op jit(solution)/shard_map/all_gather | solution.py:75
  11.5 209.2 %all-gather.5.cloned.1.call-start = ((), (), s32[]{:S(2)}) async-start(), calls=%async_computation.1 | async-start | bytes 2662400 | tf_op jit(solution)/shard_map/all_gather | solution.py:81
  67.4 1.1 copy-start.1
  74.9 1.0 copy-start.2
  75.0 1.1 copy-start.4
  76.1 1.3 copy-start.3
  78.8 9.1 %collective-permute-start = (bf16[2,32,640]{2,1,0:T(8,128)(2,1)S(1)}, bf16[2,32,640]{2,1,0:T(8,128)(2,1)}, u32[]{:S(2)}, u32[]{:S(2)}) collective-permute-start(bf16[2,32,640]{2,1,0:T(8,128)(2,1)S(1)} %get-tuple-element.9), channel_id=1, source_target_pairs={{0,8},{8,16},{16,24},{24,32},{32,40},{40,48},{48,56},{56,64},{64,7... | collective-permute-start | bytes 245768 | tf_op jit(solution)/shard_map/ppermute | solution.py:18
  82.6 10.0 %collective-permute-start.1 = (bf16[2,32,640]{2,1,0:T(8,128)(2,1)S(1)}, bf16[2,32,640]{2,1,0:T(8,128)(2,1)S(1)}, u32[]{:S(2)}, u32[]{:S(2)}) collective-permute-start(bf16[2,32,640]{2,1,0:T(8,128)(2,1)S(1)} %get-tuple-element.10), channel_id=1, source_target_pairs={{8,0},{16,8},{24,16},{32,24},{40,32},{48,40},{56,48},{64,56},{72,6... | collective-permute-start | bytes 245768 | tf_op jit(solution)/shard_map/ppermute | solution.py:20
  245.2 1.0 copy-start.5
Sparse Core Ops, SparseCore 0:
  11.6 47.7 all-gather.2
  78.8 141.8 all-gather.4
where the time goes:
time: 258 us; the launch traced here: 254 us
  waiting for transfers between devices  172 us (67%)
  local copies, waits for them, and re-layouts  34.5 us (13%)
  matrix products  14.6 us (6%)
  other arithmetic  14.1 us (5%)
  between operations  13.6 us (5%)
  starting transfers between devices  5.24 us (2%)
    all_gather x1, waiting for transfers between devices, body(): anchors = lax.all_gather(key_value[0:1], 'clip', axis=0, tiled=True)  124 us
    all_gather x1, waiting for transfers between devices, body(): lax.all_gather(packed[..., inner_width:], 'space', axis=1, tiled=True)  47.6 us
    concatenate x1, other arithmetic, body(): keys_all = jnp.concatenate([context, anchors], axis=0)  10.6 us
    all_gather x1, local copies, waits for them, and re-layouts, body(): anchors = lax.all_gather(key_value[0:1], 'clip', axis=0, tiled=True)  6.71 us
    slice x2, local copies, waits for them, and re-layouts, attend_space(): key_value[..., :inner_width]  6.43 us
  transfers between devices with their start and end apart: 4, of which 2 were waited for; matrix products, arithmetic and copies ran while one was open for 5% of the time, Pallas kernels for 0%

commit v1 on v0

v1 whole, which is shorter than its diff:
```python
import jax
import jax.numpy as jnp
from jax import lax
from jax.experimental import pallas as pl
from jax.experimental.pallas import tpu as pltpu
from jax.sharding import PartitionSpec as P

MESH = pl.DeviceIdType.MESH
HEADS = 5
NZ, NY, NX = 2, 8, 4
N_CLIP = NZ * NY * NX
NS = 8
FRAMES = 8
ROWS = 32
HALF = 16
C = 640
INNER = 320
WIDE = 384
COPIES = 112
NEG = -1e30
BF = jnp.bfloat16
F32 = jnp.float32


def wrap(value, count):
    return lax.rem(value + 2 * count, count)


def normalize(values):
    wide = values.astype(F32)
    center = wide - jnp.mean(wide, axis=-1, keepdims=True)
    spread = jnp.mean(center * center, axis=-1, keepdims=True)
    return (center * lax.rsqrt(spread + 1e-05)).astype(BF)


def dot(a, b):
    return jnp.dot(a, b, preferred_element_type=F32)


def dot_t(a, b):
    return lax.dot_general(a, b, (((1,), (1,)), ((), ())), preferred_element_type=F32)


def low_lanes(rows):
    return lax.broadcasted_iota(jnp.int32, (rows, 128), 1) < 64


def head_queries(qkv):
    low = low_lanes(qkv.shape[0])
    tiles = []
    for h in range(HEADS):
        tile = qkv[:, 128 * (h // 2):128 * (h // 2) + 128].astype(F32) * 0.125
        keep = low if h % 2 == 0 else jnp.logical_not(low)
        tiles.append(jnp.where(keep, tile, 0.0).astype(BF))
    return tiles


def side_by_side(heads):
    low = low_lanes(heads[0].shape[0])
    return jnp.concatenate(
        [
            jnp.where(low, 0.0, heads[0]),
            jnp.where(low, heads[1], heads[2]),
            jnp.where(low, heads[3], heads[4]),
        ],
        axis=1,
    )


def attend_space(queries, kv):
    heads = []
    for h in range(HEADS):
        kt, vt = 128 * (h // 2), 128 * (2 + (h + 1) // 2)
        scores = dot_t(queries[h], kv[:, kt:kt + 128])
        p = jnp.exp(scores - jnp.max(scores, axis=-1, keepdims=True))
        total = jnp.sum(p, axis=-1, keepdims=True)
        heads.append(dot(p.astype(BF), kv[:, vt:vt + 128]) / total)
    return side_by_side(heads).astype(BF)


def kernel(lat_h, wsq_h, wso_h, wtq_h, wto_h, out_ref,
           lat, wsq, wso, wtq, wto, f0, fr, kvs, q0, sa_out, sa_in, anc, tkv, prev, nxt,
           spat, qm, acc, top, tot, tatt, lsem, ssem, rsem):
    clip = lax.axis_index("clip")
    s = lax.axis_index("space")
    zh, y, x = clip // (NY * NX), (clip // NX) % NY, clip % NX
    zl, core = s // 2, s % 2

    def at_clip(z_, y_, x_):
        return {"clip": (z_ * NY + y_) * NX + x_, "space": s}

    def at_space(s_):
        return {"clip": clip, "space": s_}

    partner = at_clip(1 - zh, y, x)
    x_peer = {d: at_clip(zh, y, wrap(x + d, NX)) for d in (1, 2, 3)}
    y_peer = {d: at_clip(zh, wrap(y + d, NY), x) for d in (1, -1)}
    following = {"clip": wrap(clip + 1, N_CLIP), "space": s}
    preceding = {"clip": wrap(clip - 1, N_CLIP), "space": s}

    local = []
    wso[0:64, :] = jnp.zeros((64, C), BF)
    wto[0:64, :] = jnp.zeros((64, C), BF)
    for i, (src, dst) in enumerate([
        (lat_h, lat), (wsq_h, wsq), (wso_h, wso.at[pl.ds(64, INNER)]), (wtq_h, wtq), (wto_h, wto.at[pl.ds(64, INNER)]),
    ]):
        copy = pltpu.make_async_copy(src, dst, lsem.at[i])
        copy.start()
        local.append(copy)
    barrier = pltpu.get_barrier_semaphore()
    partners = [at_space(wrap(s + d, NS)) for d in range(1, NS)]
    partners += [partner, x_peer[1], x_peer[2], x_peer[3], y_peer[1], y_peer[-1], following, preceding]
    for device in partners:
        pl.semaphore_signal(barrier, inc=1, device_id=device, device_id_type=MESH)
    local[0].wait()
    f0[s] = lat[0]
    fr[s] = lat[s]
    pl.semaphore_wait(barrier, len(partners))

    count = [0]
    sent = []

    def number():
        count[0] += 1
        return count[0] - 1

    def make(i, src, dst, device):
        return pltpu.make_async_remote_copy(
            src_ref=src, dst_ref=dst, send_sem=ssem.at[i], recv_sem=rsem.at[i], device_id=device, device_id_type=MESH
        )

    def send(i, ref, device, dst=None):
        copy = make(i, ref, ref if dst is None else dst, device)
        copy.start()
        sent.append(copy)

    def recv(i, ref, device):
        make(i, ref, ref, device).wait_recv()

    sibling = at_space(zl * 2 + 1 - core)
    same_core = {d: at_space(wrap(zl + d, 4) * 2 + core) for d in (1, 2, 3)}
    mine = f0.at[s]
    n_direct = {d: number() for d in (1, 2, 3)}
    n_relay = {d: number() for d in (1, 2, 3)}
    n_sib = number()
    for d in (2, 1, 3):
        send(n_direct[d], mine, same_core[d])
    send(n_sib, mine, sibling)
    for d in (1, 3, 2):
        slot = f0.at[wrap(zl - d, 4) * 2 + core]
        recv(n_direct[d], slot, same_core[d])
        send(n_relay[d], slot, sibling)

    n_frame = {d: number() for d in range(1, NS)}
    n_back = {d: number() for d in range(1, NS)}

    conditional = []

    def send_if(cond, i, src, device, dst):
        copy = make(i, src, dst, device)

        @pl.when(cond)
        def _():
            copy.start()

        conditional.append((cond, copy))

    for d in range(1, NS):
        owner = wrap(s + d, NS)
        send_if(owner != 0, n_frame[d], lat.at[owner], at_space(owner), fr.at[s])

    recv(n_sib, f0.at[zl * 2 + 1 - core], sibling)
    for d in (1, 3, 2):
        recv(n_relay[d], f0.at[wrap(zl - d, 4) * 2 + 1 - core], sibling)

    def temporal_rows(latent, attn, first, frames):
        rows = frames * ROWS
        spatial = (latent.astype(F32) + dot(attn, wso[...])).astype(BF)
        spat[pl.ds(first, frames)] = spatial.reshape(frames, ROWS, C)
        qkv = dot(normalize(spatial), wtq[...]).astype(BF)
        kv = qkv[:, INNER:]
        tkv[pl.ds(first, frames)] = kv.reshape(frames, ROWS, 2 * INNER)
        for h, tile in enumerate(head_queries(qkv)):
            tile = tile.reshape(frames, ROWS, 128)
            for g in range(2):
                qm[g, h, pl.ds(first, frames)] = tile[:, HALF * g:HALF * g + HALF]
        return kv

    local[1].wait()
    qkv0 = dot(normalize(f0[...].reshape(NS * ROWS, C)), wsq[...]).astype(BF)
    q0[...] = qkv0[:, :WIDE].reshape(NS, ROWS, WIDE)
    mixed0 = attend_space(head_queries(q0[s]), qkv0[:, INNER:])
    for copy in local[2:]:
        copy.wait()
    kv0 = temporal_rows(lat[0], mixed0, 0, 1)
    anc[0, y, NX * zh + x] = kv0[:HALF]
    anc[1, NZ * x + zh, y] = kv0[HALF:]

    planes = (zh, 1 - zh)
    n_za, n_zb = number(), number()
    n_xa = {(p, d): number() for p in range(2) for d in (1, 2, 3)}
    n_ya = {(p, k, d): number() for p in range(2) for k in range(4) for d in (1, -1)}
    n_yb = {(p, k, d): number() for p in range(2) for k in range(4) for d in (1, -1)}
    n_xb = {(p, k, d): number() for p in range(2) for k in range(2) for d in (1, -1)}

    def send_xa(p):
        for d in (2, 1, 3):
            send(n_xa[p, d], anc.at[0, y, NX * planes[p] + x], x_peer[d])

    def recv_xa(p):
        for d in (1, 3, 2):
            recv(n_xa[p, d], anc.at[0, y, NX * planes[p] + wrap(x - d, NX)], x_peer[d])

    def row_a(p, yy, k, d):
        if k < 3:
            return anc.at[0, yy, pl.ds(NX * planes[p], NX)]
        return anc.at[0, yy, pl.ds(NX * planes[p] + (0 if d == 1 else 2), 2)]

    def send_ya(p, k):
        for d in (1, -1):
            send(n_ya[p, k, d], row_a(p, wrap(y - d * k, NY), k, d), y_peer[d])

    def recv_ya(p, k):
        for d in (1, -1):
            recv(n_ya[p, k, d], row_a(p, wrap(y - d * (k + 1), NY), k, d), y_peer[d])

    def ways_b(p, k):
        return (1, -1) if k < 3 else ((1,) if p == 0 else (-1,))

    def send_yb(p, k):
        for d in ways_b(p, k):
            send(n_yb[p, k, d], anc.at[1, NZ * x + planes[p], wrap(y - d * k, NY)], y_peer[d])

    def recv_yb(p, k):
        for d in ways_b(p, k):
            recv(n_yb[p, k, d], anc.at[1, NZ * x + planes[p], wrap(y - d * (k + 1), NY)], y_peer[d])

    def col_b(p, xx, k, d):
        if k == 0:
            return anc.at[1, NZ * xx + planes[p]]
        return anc.at[1, NZ * xx + planes[p], pl.ds(0 if d == 1 else 4, 4)]

    def send_xb(p, k):
        for d in (1, -1):
            send(n_xb[p, k, d], col_b(p, wrap(x - d * k, NX), k, d), x_peer[1 if d == 1 else 3])

    def recv_xb(p, k):
        for d in (1, -1):
            recv(n_xb[p, k, d], col_b(p, wrap(x - d * (k + 1), NX), k, d), x_peer[1 if d == 1 else 3])

    send(n_za, anc.at[0, y, NX * zh + x], partner)
    send(n_zb, anc.at[1, NZ * x + zh, y], partner)
    send_yb(0, 0)
    send_xa(0)

    recv_xa(0)
    send_ya(0, 0)
    recv_yb(0, 0)
    send_yb(0, 1)
    recv(n_za, anc.at[0, y, NX * (1 - zh) + x], partner)
    send_xa(1)
    recv(n_zb, anc.at[1, NZ * x + 1 - zh, y], partner)
    send_yb(1, 0)
    recv_yb(0, 1)
    send_yb(0, 2)
    recv_xa(1)
    send_ya(1, 0)
    recv_yb(1, 0)
    send_yb(1, 1)
    recv_yb(0, 2)
    send_yb(0, 3)
    recv_yb(1, 1)
    send_yb(1, 2)

    @pl.when(s != 0)
    def _():
        for d in range(1, NS):
            recv(n_frame[d], fr.at[wrap(s - d, NS)], at_space(wrap(s + d, NS)))
        qkv = dot(normalize(fr[...].reshape(NS * ROWS, C)), wsq[...]).astype(BF)
        kvs[...] = qkv[:, INNER:]
        mixed = attend_space(head_queries(qkv), kvs[...])
        sa_out[...] = mixed.reshape(NS, ROWS, WIDE)
        sa_in[s] = sa_out[s]

    for d in range(1, NS):
        there = wrap(s + d, NS)
        send_if(s != 0, n_back[d], sa_out.at[there], at_space(there), sa_in.at[s])

    recv_yb(0, 3)
    send_xb(0, 0)
    recv_ya(0, 0)
    send_ya(0, 1)
    recv_yb(1, 2)
    send_yb(1, 3)
    recv_ya(1, 0)
    send_ya(1, 1)

    for d in range(1, NS):
        owner = wrap(s - d, NS)

        @pl.when(owner != 0)
        def _():
            recv(n_back[d], sa_in.at[owner], at_space(owner))

    rest = FRAMES - 1
    temporal_rows(
        lat[1:].reshape(rest * ROWS, C), sa_in[1:].reshape(rest * ROWS, WIDE), 1, rest
    )
    n_next, n_prev = number(), number()
    send(n_next, tkv.at[pl.ds(FRAMES - 2, 2)], following, prev)
    send(n_prev, tkv.at[pl.ds(0, 2)], preceding, nxt)

    recv_yb(1, 3)
    send_xb(1, 0)
    recv_ya(0, 1)
    send_ya(0, 2)

    def same_position(keys):
        rows = lax.broadcasted_iota(jnp.int32, (HEADS * FRAMES * HALF, keys), 0) % HALF
        return rows == lax.broadcasted_iota(jnp.int32, (HEADS * FRAMES * HALF, keys), 1) % HALF

    block = FRAMES * HALF

    def attend(g, load, keys, allowed=None, start=False):
        queries = qm[g].reshape(HEADS * block, 128)
        tiles = [load(t) for t in range(5)]
        scores = jnp.concatenate(
            [
                dot_t(queries[:2 * block], tiles[0]),
                dot_t(queries[2 * block:4 * block], tiles[1]),
                dot_t(queries[4 * block:], tiles[2]),
            ],
            axis=0,
        )
        mask = same_position(keys)
        if allowed is not None:
            mask = jnp.logical_and(mask, allowed)
        scores = jnp.where(mask, scores, NEG)
        high = jnp.max(scores, axis=-1, keepdims=True)
        if not start:
            high = jnp.maximum(high, top[g])
        p = jnp.exp(scores - high)
        total = jnp.sum(p, axis=-1, keepdims=True)
        p = p.astype(BF)
        out = jnp.concatenate(
            [dot(p[:block], tiles[2]), dot(p[block:3 * block], tiles[3]), dot(p[3 * block:], tiles[4])], axis=0
        )
        if not start:
            shrink = jnp.exp(top[g] - high)
            total = total + tot[g] * shrink
            out = out + acc[g] * shrink
        top[g] = high
        tot[g] = total
        acc[g] = out

    def lanes(t):
        return pl.ds(128 * t, 128)

    def window(g):
        at = pl.ds(pl.multiple_of(HALF * g, HALF), HALF)

        def load(t):
            pieces = [r[:, at, lanes(t)] for r in (tkv, prev, nxt)]
            return jnp.concatenate([r.reshape(r.shape[0] * HALF, 128) for r in pieces], axis=0)
        return load

    def attend_window(g):
        keys = (FRAMES + 4) * HALF
        key = lax.broadcasted_iota(jnp.int32, (HEADS * block, keys), 1)
        first = jnp.where(clip > 0, block, block + 2 * HALF)
        last = jnp.where(clip < N_CLIP - 1, block + 4 * HALF, block + 2 * HALF)
        attend(g, window(g), keys, allowed=(key < block) | ((key >= first) & (key < last)))

    def attend_anchors(g, c, start=False):
        column = NZ * wrap(x + (0, 1, -1, 2)[c], NX)
        one = jnp.where(g == 0, wrap(y - c, NY), column)
        two = jnp.where(g == 0, wrap(y + c + 1, NY), column + 1)

        def load(t):
            return jnp.concatenate([anc[g, r, :, :, lanes(t)].reshape(block, 128) for r in (one, two)], axis=0)
        attend(g, load, 2 * block, start=start)

    def both(body, *args):
        def run(g, carry):
            body(g, *args)
            return carry
        lax.fori_loop(0, 2, run, 0)

    recv_ya(1, 1)
    send_ya(1, 2)
    recv_xb(0, 0)
    send_xb(0, 1)
    both(attend_anchors, 0, True)
    recv_ya(0, 2)
    send_ya(0, 3)
    recv_xb(1, 0)
    send_xb(1, 1)
    recv_ya(1, 2)
    send_ya(1, 3)
    both(attend_anchors, 1)
    recv(n_next, prev, preceding)
    recv(n_prev, nxt, following)
    both(attend_window)
    both(attend_anchors, 2)
    recv_ya(0, 3)
    recv_ya(1, 3)
    recv_xb(0, 1)
    recv_xb(1, 1)
    both(attend_anchors, 3)

    for g in range(2):
        mixed = acc[g] / tot[g]
        mixed = side_by_side([mixed[h * block:(h + 1) * block] for h in range(HEADS)]).astype(BF)
        tatt[:, g] = mixed.reshape(FRAMES, HALF, WIDE)
    update = dot(tatt[...].reshape(FRAMES * ROWS, WIDE), wto[...])
    out = (spat[...].reshape(FRAMES * ROWS, C).astype(F32) + update).astype(BF)
    out_ref[...] = out.reshape(FRAMES, ROWS, C)

    for copy in sent:
        copy.wait_send()
    for cond, copy in conditional:
        @pl.when(cond)
        def _():
            copy.wait_send()
    assert count[0] <= COPIES


def step(latent, spatial_qkv, spatial_out, temporal_qkv, temporal_out):
    vmem = pltpu.VMEM
    tokens = FRAMES * HALF
    return pl.pallas_call(
        kernel,
        out_shape=jax.ShapeDtypeStruct(latent.shape, BF),
        in_specs=[pl.BlockSpec(memory_space=pl.ANY)] * 5,
        out_specs=pl.BlockSpec(memory_space=pltpu.VMEM),
        scratch_shapes=[
            vmem((FRAMES, ROWS, C), BF),
            vmem((C, 3 * INNER), BF),
            vmem((WIDE, C), BF),
            vmem((C, 3 * INNER), BF),
            vmem((WIDE, C), BF),
            vmem((NS, ROWS, C), BF),
            vmem((NS, ROWS, C), BF),
            vmem((NS * ROWS, 2 * INNER), BF),
            vmem((NS, ROWS, WIDE), BF),
            vmem((NS, ROWS, WIDE), BF),
            vmem((FRAMES, ROWS, WIDE), BF),
            vmem((2, 8, 8, HALF, 2 * INNER), BF),
            vmem((FRAMES, ROWS, 2 * INNER), BF),
            vmem((2, ROWS, 2 * INNER), BF),
            vmem((2, ROWS, 2 * INNER), BF),
            vmem((FRAMES, ROWS, C), BF),
            vmem((2, HEADS, FRAMES, HALF, 128), BF),
            vmem((2, HEADS * tokens, 128), F32),
            vmem((2, HEADS * tokens, 1), F32),
            vmem((2, HEADS * tokens, 1), F32),
            vmem((FRAMES, 2, HALF, WIDE), BF),
            pltpu.SemaphoreType.DMA((5,)),
            pltpu.SemaphoreType.DMA((COPIES,)),
            pltpu.SemaphoreType.DMA((COPIES,)),
        ],
        compiler_params=pltpu.CompilerParams(
            collective_id=0, has_side_effects=True, vmem_limit_bytes=40 * 1024 * 1024
        ),
        name="denoise",
    )(latent, spatial_qkv, spatial_out, temporal_qkv, temporal_out)


def solution(mesh):
    in_specs = (P("clip", "space", None), P(), P(), P(), P())
    out_specs = P("clip", "space", None)
    return jax.shard_map(step, mesh=mesh, in_specs=in_specs, out_specs=out_specs, check_vma=False)
```

time: 258 us -> 68.7 us (0.27); the launches traced: 254 us -> 68.5 us
  waiting for transfers between devices: 172 us -> 0 us
  Pallas kernels: 0 us -> 63.4 us
  local copies, waits for them, and re-layouts: 34.5 us -> 5 us
  matrix products: 14.6 us -> 0 us
  other arithmetic: 14.1 us -> 0 us
  between operations: 13.6 us -> 0.06 us
  starting transfers between devices: 5.24 us -> 0 us
    all_gather x2 -> x0, waiting for transfers between devices: 172 us -> none  [the longest x1 124 us: body(): anchors = lax.all_gather(key_value[0:1], 'clip', axis=0, tiled=True)]
    pallas_call x0 -> x1, Pallas kernels: none -> 63.4 us  [step(): pl.pallas_call(kernel, out_shape=jax.ShapeDtypeStruct(latent.shape, BF),...]
    slice x11 -> x0, local copies, waits for them, and re-layouts: 15.3 us -> none  [the longest x2 6.43 us: attend_space(): key_value[..., :inner_width]]
    dot_general x8 -> x0, matrix products: 14.6 us -> none  [the longest x1 4.39 us: attend_space(): jnp.einsum('fhqk,fkhd->fqhd', weights, value_heads, preferred_element_typ...]
    concatenate x1 -> x0, other arithmetic: 10.6 us -> none  [body(): keys_all = jnp.concatenate([context, anchors], axis=0)]
    ppermute x2 -> x0, local copies, waits for them, and re-layouts: 8.23 us -> none  [the longest x1 4.6 us: padded(): lax.ppermute(tail, axis, [(i, (i + 1) % count) for i in range(ends)])]
    all_gather x1 -> x0, local copies, waits for them, and re-layouts: 6.71 us -> none  [body(): anchors = lax.all_gather(key_value[0:1], 'clip', axis=0, tiled=True)]
    ppermute x2 -> x0, starting transfers between devices: 5.2 us -> none  [the longest x1 3.74 us: padded(): lax.ppermute(tail, axis, [(i, (i + 1) % count) for i in range(ends)])]
  transfers between devices with their start and end apart: 4 -> 0, of which waited for: 2 -> 0; matrix products, arithmetic and copies ran while one was open for 5% -> 0% of each run, Pallas kernels for 0% -> 0%
where the time goes in v1:
time: 68.7 us; the launch traced here: 68.5 us
  Pallas kernels  63.4 us (92%)
  local copies, waits for them, and re-layouts  5 us (7%)
    pallas_call x1, Pallas kernels, step(): pl.pallas_call(kernel, out_shape=jax.ShapeDtypeStruct(latent.shape, BF),...  63.4 us
    unnamed x9, local copies, waits for them, and re-layouts  5 us

profile of v1, /device:TPU:1, one launch (start us, length us, event | category | flops | bytes accessed | tf_op | source)
XLA Modules:
  0.0 68.5 jit_solution(12811214634577968222)
XLA Ops:
  0.0 1.6 %copy.6.wsq_h = bf16[640,960]{1,0:T(8,128)(2,1)S(1)} copy(bf16[640,960]{0,1:T(8,128)(2,1)} %param.6) | data formatting | bytes 2457600 | tf_op args[1]
  1.6 0.0 copy-start
  1.6 0.0 copy-start.1
  1.6 1.7 %copy.7.wtq_h = bf16[640,960]{1,0:T(8,128)(2,1)S(1)} copy(bf16[640,960]{0,1:T(8,128)(2,1)} %param.8) | data formatting | bytes 2457600 | tf_op args[3]
  3.3 0.0 copy-done
  3.3 0.0 copy-done.1
  3.4 0.0 copy-start.2
  3.4 1.0 %copy-done.2 = bf16[8,32,640]{2,1,0:T(8,128)(2,1)S(1)} copy-done((bf16[8,32,640]{2,1,0:T(8,128)(2,1)S(1)}, bf16[8,32,640]{2,1,0:T(8,128)(2,1)}, u32[]{:S(2)}) %copy-start.2) | copy-done | bytes 327704
  4.3 63.4 %denoise.1 = bf16[8,32,640]{2,1,0:T(8,128)(2,1)S(1)} custom-call(bf16[8,32,640]{2,1,0:T(8,128)(2,1)S(1)} %copy-done.2, bf16[640,960]{1,0:T(8,128)(2,1)S(1)} %copy.6.wsq_h, bf16[320,640]{1,0:T(8,128)(2,1)S(1)} %copy-done, bf16[640,960]{1,0:T(8,128)(2,1)S(1)} %copy.7.wtq_h, bf16[320,640]{1,0:T(8,128)(2,1)S(1)} %copy-done.1), custom_call_target="tpu_custom_call" | custom-call | tf_op jit(solution)/shard_map/denoise/pallas_call | solution.py:431
  67.8 0.7 %copy.9 = bf16[8,32,640]{2,1,0:T(8,128)(2,1)} copy(bf16[8,32,640]{2,1,0:T(8,128)(2,1)S(1)} %denoise.1) | data formatting | bytes 655360
Async XLA Ops:
  1.6 1.7 %copy-start = (bf16[320,640]{1,0:T(8,128)(2,1)S(1)}, bf16[320,640]{1,0:T(8,128)(2,1)}, u32[]{:S(2)}) copy-start(bf16[320,640]{1,0:T(8,128)(2,1)} %wso_h.1) | copy-start | bytes 1228804
  1.6 1.7 %copy-start.1 = (bf16[320,640]{1,0:T(8,128)(2,1)S(1)}, bf16[320,640]{1,0:T(8,128)(2,1)}, u32[]{:S(2)}) copy-start(bf16[320,640]{1,0:T(8,128)(2,1)} %wto_h.1) | copy-start | bytes 1228804
  3.4 1.0 %copy-start.2 = (bf16[8,32,640]{2,1,0:T(8,128)(2,1)S(1)}, bf16[8,32,640]{2,1,0:T(8,128)(2,1)}, u32[]{:S(2)}) copy-start(bf16[8,32,640]{2,1,0:T(8,128)(2,1)} %lat_h.1) | copy-start | bytes 983044

commit v2 on v1

v2 whole, which is shorter than its diff:
```python
import jax
import jax.numpy as jnp
from jax import lax
from jax.experimental import pallas as pl
from jax.experimental.pallas import tpu as pltpu
from jax.sharding import PartitionSpec as P

MESH = pl.DeviceIdType.MESH
HEADS = 5
NZ, NY, NX = 2, 8, 4
N_CLIP = NZ * NY * NX
NS = 8
FRAMES = 8
ROWS = 32
HALF = 16
C = 640
INNER = 320
WIDE = 384
COPIES = 112
NEG = -1e30
BF = jnp.bfloat16
F32 = jnp.float32


def wrap(value, count):
    return lax.rem(value + 2 * count, count)


def normalize(values):
    wide = values.astype(F32)
    center = wide - jnp.mean(wide, axis=-1, keepdims=True)
    spread = jnp.mean(center * center, axis=-1, keepdims=True)
    return (center * lax.rsqrt(spread + 1e-05)).astype(BF)


def dot(a, b):
    return jnp.dot(a, b, preferred_element_type=F32)


def dot_t(a, b):
    return lax.dot_general(a, b, (((1,), (1,)), ((), ())), preferred_element_type=F32)


def low_lanes(rows):
    return lax.broadcasted_iota(jnp.int32, (rows, 128), 1) < 64


def head_queries(queries):
    low = low_lanes(queries.shape[0])
    tiles = []
    for h in range(HEADS):
        tile = queries[:, 128 * (h // 2):128 * (h // 2) + 128].astype(BF).astype(F32) * 0.125
        keep = low if h % 2 == 0 else jnp.logical_not(low)
        tiles.append(jnp.where(keep, tile, 0.0).astype(BF))
    return tiles


def side_by_side(heads):
    low = low_lanes(heads[0].shape[0])
    return jnp.concatenate(
        [
            jnp.where(low, 0.0, heads[0]),
            jnp.where(low, heads[1], heads[2]),
            jnp.where(low, heads[3], heads[4]),
        ],
        axis=1,
    )


def attend_space(queries, kv):
    heads = []
    for h in range(HEADS):
        kt, vt = 128 * (h // 2), 128 * (2 + (h + 1) // 2)
        scores = dot_t(queries[h], kv[:, kt:kt + 128])
        p = jnp.exp(scores - jnp.max(scores, axis=-1, keepdims=True))
        total = jnp.sum(p, axis=-1, keepdims=True)
        heads.append(dot(p.astype(BF), kv[:, vt:vt + 128]) / total)
    return side_by_side(heads).astype(BF)


def kernel(lat_h, wsq_h, wso_h, wtq_h, wto_h, out_ref,
           lat, wsq, wso, wtq, wto, f0, fr, kvs, sa_out, sa_in, anc, tkv, prev, nxt,
           spat, qm, acc, top, tot, tatt, lsem, ssem, rsem):
    clip = lax.axis_index("clip")
    s = lax.axis_index("space")
    zh, y, x = clip // (NY * NX), (clip // NX) % NY, clip % NX
    zl, core = s // 2, s % 2

    def at_clip(z_, y_, x_):
        return {"clip": (z_ * NY + y_) * NX + x_, "space": s}

    def at_space(s_):
        return {"clip": clip, "space": s_}

    partner = at_clip(1 - zh, y, x)
    x_peer = {d: at_clip(zh, y, wrap(x + d, NX)) for d in (1, 2, 3)}
    y_peer = {d: at_clip(zh, wrap(y + d, NY), x) for d in range(1, NY)}
    following = {"clip": wrap(clip + 1, N_CLIP), "space": s}
    preceding = {"clip": wrap(clip - 1, N_CLIP), "space": s}

    barrier = pltpu.get_barrier_semaphore()
    partners = [at_space(wrap(s + d, NS)) for d in range(1, NS)]
    partners += [partner] + [x_peer[d] for d in (1, 2, 3)] + [y_peer[d] for d in range(1, NY)] + [following, preceding]
    for device in partners:
        pl.semaphore_signal(barrier, inc=1, device_id=device, device_id_type=MESH)
    local = []

    def fetch(*pairs):
        for src, dst in pairs:
            copy = pltpu.make_async_copy(src, dst, lsem.at[len(local)])
            copy.start()
            local.append(copy)

    fetch((lat_h, lat))
    wso[0:64, :] = jnp.zeros((64, C), BF)
    wto[0:64, :] = jnp.zeros((64, C), BF)
    pl.semaphore_wait(barrier, len(partners))

    count = [0]
    sent = []

    def number():
        count[0] += 1
        return count[0] - 1

    def make(i, src, dst, device):
        return pltpu.make_async_remote_copy(
            src_ref=src, dst_ref=dst, send_sem=ssem.at[i], recv_sem=rsem.at[i], device_id=device, device_id_type=MESH
        )

    def send(i, ref, device, dst=None):
        copy = make(i, ref, ref if dst is None else dst, device)
        copy.start()
        sent.append(copy)

    def recv(i, ref, device):
        make(i, ref, ref, device).wait_recv()

    sibling = at_space(zl * 2 + 1 - core)
    same_core = {d: at_space(wrap(zl + d, 4) * 2 + core) for d in (1, 2, 3)}
    mine = lat_h.at[0]
    n_direct = {d: number() for d in (1, 2, 3)}
    n_relay = {d: number() for d in (1, 2, 3)}
    n_sib = number()
    for d in (2, 1, 3):
        send(n_direct[d], mine, same_core[d], f0.at[s])
    send(n_sib, mine, sibling, f0.at[s])
    fetch((wsq_h, wsq), (wso_h, wso.at[pl.ds(64, INNER)]), (wtq_h, wtq), (wto_h, wto.at[pl.ds(64, INNER)]))
    local[0].wait()
    f0[s] = lat[0]
    fr[s] = lat[s]
    for d in (1, 3, 2):
        slot = f0.at[wrap(zl - d, 4) * 2 + core]
        recv(n_direct[d], slot, same_core[d])
        send(n_relay[d], slot, sibling)

    n_frame = {d: number() for d in range(1, NS)}
    n_back = {d: number() for d in range(1, NS)}

    conditional = []

    def send_if(cond, i, src, device, dst):
        copy = make(i, src, dst, device)

        @pl.when(cond)
        def _():
            copy.start()

        conditional.append((cond, copy))

    for d in range(1, NS):
        owner = wrap(s + d, NS)
        send_if(owner != 0, n_frame[d], lat_h.at[owner], at_space(owner), fr.at[s])

    recv(n_sib, f0.at[zl * 2 + 1 - core], sibling)
    for d in (1, 3, 2):
        recv(n_relay[d], f0.at[wrap(zl - d, 4) * 2 + 1 - core], sibling)

    def temporal_rows(latent, attn, first, frames):
        rows = frames * ROWS
        spatial = (latent.astype(F32) + dot(attn, wso[...])).astype(BF)
        spat[pl.ds(first, frames)] = spatial.reshape(frames, ROWS, C)
        normed = normalize(spatial)
        kv = dot_t(normed, wtq[INNER:]).astype(BF)
        tkv[pl.ds(first, frames)] = kv.reshape(frames, ROWS, 2 * INNER)
        return kv, normed

    def temporal_queries(normed, first, frames):
        for h, tile in enumerate(head_queries(dot_t(normed, wtq[:WIDE]))):
            tile = tile.reshape(frames, ROWS, 128)
            for g in range(2):
                qm[g, h, pl.ds(first, frames)] = tile[:, HALF * g:HALF * g + HALF]

    local[1].wait()
    queries0 = head_queries(dot_t(normalize(lat[0]), wsq[:WIDE]))
    kvs[...] = dot_t(normalize(f0[...].reshape(NS * ROWS, C)), wsq[INNER:]).astype(BF)
    mixed0 = attend_space(queries0, kvs)
    for copy in local[2:]:
        copy.wait()
    kv0, normed0 = temporal_rows(lat[0], mixed0, 0, 1)
    anc[0, y // 2, (y % 2) * NX + x] = kv0[:HALF]
    anc[1, NZ * x, y] = kv0[HALF:]

    def cell(part, xx, yy):
        if part == 0:
            return anc.at[0, yy // 2, (yy % 2) * NX + xx]
        if part == 1:
            return anc.at[0, NX + xx, yy]
        return anc.at[1, NZ * xx + part - 2, yy]

    def column(part, xx, *half):
        ref = anc.at[0, NX + xx] if part == 1 else anc.at[1, NZ * xx + part - 2]
        return ref.at[pl.ds(*half)] if half else ref

    def line(yy, k, d):
        start = (yy % 2) * NX
        return anc.at[0, yy // 2, pl.ds(start, NX) if k < 3 else pl.ds(start + (0 if d == 1 else 2), 2)]

    parts = (2, 1, 3)
    n_z = {part: number() for part in (1, 3)}
    n_xa = {d: number() for d in (1, 2, 3)}
    n_ya = {(k, d): number() for k in range(4) for d in (1, -1)}
    n_yb = {(part, d): number() for part in parts for d in range(1, NY)}
    n_xb = {(part, d): number() for part in parts for d in (1, 3)}
    n_xc = {(part, d): number() for part in parts for d in (1, 3)}

    def send_ya(*steps):
        for k in steps:
            for d in (1, -1):
                hop = (1, 2, 1, 2)[k]
                send(n_ya[k, d], line(wrap(y - d * (k + 1 - hop), NY), k, d), y_peer[d * hop % NY])

    def recv_ya(*steps):
        for k in steps:
            for d in (1, -1):
                recv(n_ya[k, d], line(wrap(y - d * (k + 1), NY), k, d), y_peer[d % NY])

    def send_xb(part, yy):
        block = cell(part, x, yy)
        for d in (1, 3):
            make(n_xb[part, d], block, block, x_peer[d]).start()

    def spread(part):
        for d in (1, 7, 2, 6, 3, 5, 4):
            send(n_yb[part, d], cell(part, x, y), y_peer[d])
        send_xb(part, y)

    def pass_on(part):
        for d in (1, 7, 2, 6, 3, 5, 4):
            yy = wrap(y - d, NY)
            recv(n_yb[part, d], cell(part, x, yy), y_peer[d])
            send_xb(part, yy)
        for d in (1, 3):
            sent.append(make(n_xb[part, d], column(part, x), column(part, x), x_peer[d]))

    def cross(part):
        for d in (1, 3):
            recv(n_xb[part, d], column(part, wrap(x - d, NX)), x_peer[d])
            send(n_xc[part, d], column(part, wrap(x - d, NX), 0 if d == 1 else 4, 4), x_peer[d])

    def recv_xc(part):
        for d in (1, 3):
            recv(n_xc[part, d], column(part, wrap(x + 2, NX), 0 if d == 1 else 4, 4), x_peer[d])

    for part, source in ((1, cell(0, x, y)), (3, cell(2, x, y))):
        send(n_z[part], source, partner, cell(part, x, y))
    for d in (1, 3, 2):
        send(n_xa[d], cell(0, x, y), x_peer[d])
    spread(2)
    temporal_queries(normed0, 0, 1)
    for d in (1, 3, 2):
        recv(n_xa[d], cell(0, wrap(x - d, NX), y), x_peer[d])
    send_ya(0, 1)
    for part in (1, 3):
        recv(n_z[part], cell(part, x, y), partner)
        spread(part)

    @pl.when(s != 0)
    def _():
        for d in range(1, NS):
            recv(n_frame[d], fr.at[wrap(s - d, NS)], at_space(wrap(s + d, NS)))
        normed = normalize(fr[...].reshape(NS * ROWS, C))
        kvs[...] = dot_t(normed, wsq[INNER:]).astype(BF)
        mixed = attend_space(head_queries(dot_t(normed, wsq[:WIDE])), kvs)
        sa_out[...] = mixed.reshape(NS, ROWS, WIDE)
        sa_in[s] = sa_out[s]

    for d in range(1, NS):
        there = wrap(s + d, NS)
        send_if(s != 0, n_back[d], sa_out.at[there], at_space(there), sa_in.at[s])

    pass_on(2)
    recv_ya(0, 1)
    send_ya(2, 3)
    pass_on(1)
    pass_on(3)
    cross(2)

    for d in range(1, NS):
        owner = wrap(s - d, NS)

        @pl.when(owner != 0)
        def _():
            recv(n_back[d], sa_in.at[owner], at_space(owner))

    rest = FRAMES - 1
    _, normed = temporal_rows(
        lat[1:].reshape(rest * ROWS, C), sa_in[1:].reshape(rest * ROWS, WIDE), 1, rest
    )
    n_next, n_prev = number(), number()
    send(n_next, tkv.at[pl.ds(FRAMES - 2, 2)], following, prev)
    send(n_prev, tkv.at[pl.ds(0, 2)], preceding, nxt)
    temporal_queries(normed, 1, rest)

    cross(1)
    cross(3)

    block = FRAMES * HALF
    row = lax.broadcasted_iota(jnp.int32, (HALF, 128), 0)
    lane = lax.broadcasted_iota(jnp.int32, (HALF, 128), 1)
    same = row == lane % HALF
    first = jnp.where(clip > 0, 0, 2 * HALF)
    last = jnp.where(clip < N_CLIP - 1, 4 * HALF, 2 * HALF)
    same_there = same & (lane >= first) & (lane < last)

    def attend(g, load, masks, start=False):
        queries = qm[g].reshape(HEADS * block, 128)
        tiles = [load(t) for t in range(5)]
        scores = jnp.concatenate(
            [
                dot_t(queries[:2 * block], tiles[0]),
                dot_t(queries[2 * block:4 * block], tiles[1]),
                dot_t(queries[4 * block:], tiles[2]),
            ],
            axis=0,
        )
        parts = []
        for i, mask in enumerate(masks):
            part = scores[:, 128 * i:128 * i + 128].reshape(-1, HALF, 128)
            parts.append(jnp.where(mask[None], part, NEG).reshape(HEADS * block, 128))
        high = parts[0]
        for part in parts[1:]:
            high = jnp.maximum(high, part)
        high = jnp.broadcast_to(jnp.max(high, axis=-1, keepdims=True), high.shape)
        if not start:
            high = jnp.maximum(high, top[g])
        parts = [jnp.exp(part - high) for part in parts]
        total = parts[0]
        for part in parts[1:]:
            total = total + part
        p = jnp.concatenate([part.astype(BF) for part in parts], axis=1)
        out = jnp.concatenate(
            [dot(p[:block], tiles[2]), dot(p[block:3 * block], tiles[3]), dot(p[3 * block:], tiles[4])], axis=0
        )
        if not start:
            shrink = jnp.exp(top[g] - high)
            total = total + tot[g] * shrink
            out = out + acc[g] * shrink
        top[g] = high
        tot[g] = total
        acc[g] = out

    def lanes(t):
        return pl.ds(128 * t, 128)

    def window(g, t):
        at = pl.ds(pl.multiple_of(HALF * g, HALF), HALF)
        own, before, after = [r[:, at, lanes(t)].reshape(-1, 128) for r in (tkv, prev, nxt)]
        return [own, before, after, before, after]

    def anchors(g, t, c):
        beside = (wrap(x + 1, NX), wrap(x - 1, NX))
        across = wrap(x + 2, NX)
        rows_a = [
            (y // 2, NX + x),
            (NX + beside[0], NX + beside[1]),
            (wrap(y // 2 + 1, NX), wrap(y // 2 - 1, NX)),
            (wrap(y // 2 + 2, NX), NX + across),
        ][c]
        rows_b = [NZ * xx for xx in (x, beside[0], beside[1], across)][c]
        rows = [jnp.where(g == 0, rows_a[i], rows_b + i) for i in range(2)]
        return [anc[g, r, :, :, lanes(t)].reshape(block, 128) for r in rows]

    def attend_anchors(g, chunks, start=False):
        def load(t):
            return jnp.concatenate([r for c in chunks for r in anchors(g, t, c)], axis=0)
        attend(g, load, [same, same] * len(chunks), start=start)

    def attend_window(g):
        def load(t):
            return jnp.concatenate(window(g, t), axis=0)
        attend(g, load, [same, same_there])

    def both(body, *args):
        def run(g, carry):
            body(g, *args)
            return carry
        lax.fori_loop(0, 2, run, 0)

    both(attend_anchors, (0,), True)
    recv_ya(2, 3)
    both(attend_anchors, (1, 2))
    recv(n_next, prev, preceding)
    recv(n_prev, nxt, following)
    both(attend_window)
    for part in parts:
        recv_xc(part)
    both(attend_anchors, (3,))

    for g in range(2):
        mixed = acc[g] / jnp.sum(tot[g], axis=-1, keepdims=True)
        mixed = side_by_side([mixed[h * block:(h + 1) * block] for h in range(HEADS)]).astype(BF)
        tatt[:, g] = mixed.reshape(FRAMES, HALF, WIDE)
    update = dot(tatt[...].reshape(FRAMES * ROWS, WIDE), wto[...])
    out = (spat[...].reshape(FRAMES * ROWS, C).astype(F32) + update).astype(BF)
    out_ref[...] = out.reshape(FRAMES, ROWS, C)
    for copy in sent:
        copy.wait_send()
    for cond, copy in conditional:
        @pl.when(cond)
        def _():
            copy.wait_send()
    assert count[0] <= COPIES


def step(latent, spatial_qkv, spatial_out, temporal_qkv, temporal_out):
    vmem = pltpu.VMEM
    tokens = FRAMES * HALF
    return pl.pallas_call(
        kernel,
        out_shape=jax.ShapeDtypeStruct(latent.shape, BF),
        in_specs=[pl.BlockSpec(memory_space=pl.ANY)] * 5,
        out_specs=pl.BlockSpec(memory_space=pltpu.VMEM),
        scratch_shapes=[
            vmem((FRAMES, ROWS, C), BF),
            vmem((3 * INNER, C), BF),
            vmem((WIDE, C), BF),
            vmem((3 * INNER, C), BF),
            vmem((WIDE, C), BF),
            vmem((NS, ROWS, C), BF),
            vmem((NS, ROWS, C), BF),
            vmem((NS * ROWS, 2 * INNER), BF),
            vmem((NS, ROWS, WIDE), BF),
            vmem((FRAMES, ROWS, WIDE), BF),
            vmem((2, 8, 8, HALF, 2 * INNER), BF),
            vmem((FRAMES, ROWS, 2 * INNER), BF),
            vmem((2, ROWS, 2 * INNER), BF),
            vmem((2, ROWS, 2 * INNER), BF),
            vmem((FRAMES, ROWS, C), BF),
            vmem((2, HEADS, FRAMES, HALF, 128), BF),
            vmem((2, HEADS * tokens, 128), F32),
            vmem((2, HEADS * tokens, 128), F32),
            vmem((2, HEADS * tokens, 128), F32),
            vmem((FRAMES, 2, HALF, WIDE), BF),
            pltpu.SemaphoreType.DMA((5,)),
            pltpu.SemaphoreType.DMA((COPIES,)),
            pltpu.SemaphoreType.DMA((COPIES,)),
        ],
        compiler_params=pltpu.CompilerParams(
            collective_id=0, has_side_effects=True, vmem_limit_bytes=60 * 1024 * 1024
        ),
        name="denoise",
    )(latent, spatial_qkv.T, spatial_out, temporal_qkv.T, temporal_out)


def solution(mesh):
    in_specs = (P("clip", "space", None), P(), P(), P(), P())
    out_specs = P("clip", "space", None)
    return jax.shard_map(step, mesh=mesh, in_specs=in_specs, out_specs=out_specs, check_vma=False)
```

time: 68.7 us -> 59.5 us (0.87)
  Pallas kernels: 63.4 us -> 57.7 us
  local copies, waits for them, and re-layouts: 5 us -> 1.73 us
    pallas_call x1, Pallas kernels: 63.4 us -> 57.7 us  [step(): pl.pallas_call(kernel, out_shape=jax.ShapeDtypeStruct(latent.shape, BF),...]
    unnamed x9 -> x1, local copies, waits for them, and re-layouts: 5 us -> 1.73 us
where the time goes in v2:
time: 59.5 us; the launch traced here: 59.4 us
  Pallas kernels  57.7 us (97%)
  local copies, waits for them, and re-layouts  1.73 us (3%)
    pallas_call x1, Pallas kernels, step(): pl.pallas_call(kernel, out_shape=jax.ShapeDtypeStruct(latent.shape, BF),...  57.7 us
    unnamed x1, local copies, waits for them, and re-layouts  1.73 us

profile of v2, /device:TPU:1, one launch (start us, length us, event | category | flops | bytes accessed | tf_op | source)
XLA Modules:
  0.0 59.4 jit_solution(6741954616364611786)
XLA Ops:
  0.0 57.7 %denoise.1 = bf16[8,32,640]{2,1,0:T(8,128)(2,1)} custom-call(bf16[8,32,640]{2,1,0:T(8,128)(2,1)} %lat_h.1, bf16[960,640]{1,0:T(8,128)(2,1)} %bitcast.2, bf16[320,640]{1,0:T(8,128)(2,1)} %wso_h.1, bf16[960,640]{1,0:T(8,128)(2,1)} %bitcast.3, bf16[320,640]{1,0:T(8,128)(2,1)} %wto_h.1), custom_call_target="tpu_custom_call" | custom-call | tf_op jit(solution)/shard_map/denoise/pallas_call | solution.py:429
  57.7 1.7 %copy.7 = bf16[8,32,640]{2,1,0:T(8,128)(2,1)} copy(bf16[8,32,640]{2,1,0:T(8,128)(2,1)} %denoise.1) | data formatting | bytes 655360

commit v3 on v2

--- a/solution.py
+++ b/solution.py
@@ -168,10 +168,6 @@
 
         conditional.append((cond, copy))
 
-    for d in range(1, NS):
-        owner = wrap(s + d, NS)
-        send_if(owner != 0, n_frame[d], lat_h.at[owner], at_space(owner), fr.at[s])
-
     recv(n_sib, f0.at[zl * 2 + 1 - core], sibling)
     for d in (1, 3, 2):
         recv(n_relay[d], f0.at[wrap(zl - d, 4) * 2 + 1 - core], sibling)
@@ -264,6 +260,9 @@
 
     for part, source in ((1, cell(0, x, y)), (3, cell(2, x, y))):
         send(n_z[part], source, partner, cell(part, x, y))
+    for d in range(1, NS):
+        owner = wrap(s + d, NS)
+        send_if(owner != 0, n_frame[d], lat_h.at[owner], at_space(owner), fr.at[s])
     for d in (1, 3, 2):
         send(n_xa[d], cell(0, x, y), x_peer[d])
     spread(2)
@@ -310,10 +309,10 @@
     n_next, n_prev = number(), number()
     send(n_next, tkv.at[pl.ds(FRAMES - 2, 2)], following, prev)
     send(n_prev, tkv.at[pl.ds(0, 2)], preceding, nxt)
-    temporal_queries(normed, 1, rest)
 
     cross(1)
     cross(3)
+    temporal_queries(normed, 1, rest)
 
     block = FRAMES * HALF
     row = lax.broadcasted_iota(jnp.int32, (HALF, 128), 0)

time: 59.5 us -> 59.5 us (level)
  no operation moved by 1% of the time
where the time goes in v3:
time: 59.5 us; the launch traced here: 59.3 us
  Pallas kernels  57.6 us (97%)
  local copies, waits for them, and re-layouts  1.73 us (3%)
    pallas_call x1, Pallas kernels, step(): pl.pallas_call(kernel, out_shape=jax.ShapeDtypeStruct(latent.shape, BF),...  57.6 us
    unnamed x1, local copies, waits for them, and re-layouts  1.73 us

profile of v3, /device:TPU:1, one launch (start us, length us, event | category | flops | bytes accessed | tf_op | source)
XLA Modules:
  0.0 59.3 jit_solution(1372824441130943992)
XLA Ops:
  0.0 57.6 %denoise.1 = bf16[8,32,640]{2,1,0:T(8,128)(2,1)} custom-call(bf16[8,32,640]{2,1,0:T(8,128)(2,1)} %lat_h.1, bf16[960,640]{1,0:T(8,128)(2,1)} %bitcast.2, bf16[320,640]{1,0:T(8,128)(2,1)} %wso_h.1, bf16[960,640]{1,0:T(8,128)(2,1)} %bitcast.3, bf16[320,640]{1,0:T(8,128)(2,1)} %wto_h.1), custom_call_target="tpu_custom_call" | custom-call | tf_op jit(solution)/shard_map/denoise/pallas_call | solution.py:428
  57.6 1.7 %copy.7 = bf16[8,32,640]{2,1,0:T(8,128)(2,1)} copy(bf16[8,32,640]{2,1,0:T(8,128)(2,1)} %denoise.1) | data formatting | bytes 655360
